TPU v7x, 32 devices: a whole 2x2x4 slice. The times are simulated.
32 devices in a mesh: groups: 2 (over y), az: 4 (over z), rad: 2 (over x), vert: 2 (over core).
Axes of the slice: x: 2, y: 2, z: 4, core: 2. Of those that a mesh axis runs over, the one named last changes fastest.
Arguments:
- state: float32 [16, 8, 64, 512], P('groups', 'vert', 'rad', 'az'), parts along dimension 0, as said below
- orbit_shift: int32 [128], P(('groups', 'rad')), parts along dimension 0, may hold values from 0 to 511
- remap_shift: int32 [2], P('groups'), parts along dimension 0, may hold values from 0 to 511
Outputs:
- state_new: float32 [16, 8, 64, 512], P('groups', 'vert', 'rad', 'az'), parts along dimension 0
There are 2 independent parts, one for each index of `groups`. A program takes and returns all parts, laid end to end along the dimension named above; each array names one. Nothing has to cross between parts.
Inputs may be any that keep to these rules, and one draw needn't show every extreme that they name: Every cell of state has positive density and positive gas pressure.
All inputs are finite; a program needn't handle non-finite values.
Results may differ from a plain program's by a relative error of at most 0.00002.
Values sent between devices are 32-bit elements; how exact they have to be, the bound alone decides.
A program may use at most 128 MiB of HBM per device.

v0:
```python
import jax
import jax.numpy as jnp
from jax import lax
from jax.sharding import PartitionSpec as P

ADIABATIC = 5.0 / 3.0
TIME_STEP = 0.125
ROTATION = 1.0
SHEAR_RATE = 1.5


def with_halo(block, sides, width):
    for axis, dim in sides:
        count = lax.axis_size(axis)
        forward = [(i, i + 1) for i in range(count - 1)]
        forward.append((count - 1, 0))
        backward = [(target, source) for source, target in forward]
        low = lax.ppermute(
            lax.slice_in_dim(block, block.shape[dim] - width, None, axis=dim), axis, forward
        )
        high = lax.ppermute(lax.slice_in_dim(block, 0, width, axis=dim), axis, backward)
        block = jnp.concatenate([low, block, high], axis=dim)
    return block


def normal_flux(cells, normal):
    density = cells[0]
    momentum = cells[1:4]
    energy = cells[4]
    magnet = cells[5:8]
    velocity = momentum / density
    magnet_sq = jnp.sum(magnet * magnet, axis=0)
    kinetic = 0.5 * jnp.sum(momentum * velocity, axis=0)
    pressure = (ADIABATIC - 1.0) * (energy - kinetic - 0.5 * magnet_sq)
    total_pressure = pressure + 0.5 * magnet_sq
    normal_speed = velocity[normal]
    normal_field = magnet[normal]
    projection = jnp.sum(velocity * magnet, axis=0)
    pieces = [density * normal_speed]
    for component in range(3):
        term = momentum[component] * normal_speed - magnet[component] * normal_field
        if component == normal:
            term = term + total_pressure
        pieces.append(term)
    pieces.append((energy + total_pressure) * normal_speed - normal_field * projection)
    for component in range(3):
        pieces.append(magnet[component] * normal_speed - velocity[component] * normal_field)
    fast_speed = jnp.sqrt((ADIABATIC * pressure + magnet_sq) / density)
    return (jnp.stack(pieces), normal_speed, fast_speed)


def riemann_flux(left_cells, right_cells, normal):
    left_flux, left_speed, left_fast = normal_flux(left_cells, normal)
    right_flux, right_speed, right_fast = normal_flux(right_cells, normal)
    slow_bound = jnp.minimum(jnp.minimum(left_speed - left_fast, right_speed - right_fast), 0.0)
    fast_bound = jnp.maximum(jnp.maximum(left_speed + left_fast, right_speed + right_fast), 0.0)
    return (
        fast_bound * left_flux
        - slow_bound * right_flux
        + slow_bound * fast_bound * (right_cells - left_cells)
    ) / (fast_bound - slow_bound)


def advance(padded):
    flux_x = riemann_flux(padded[:, :, :-1, :], padded[:, :, 1:, :], 0)
    flux_y = riemann_flux(padded[:, :, :, :-1], padded[:, :, :, 1:], 1)
    flux_z = riemann_flux(padded[:, :-1], padded[:, 1:], 2)
    interior = padded[:, 1:-1, 1:-1, 1:-1]
    change = (
        flux_x[:, 1:-1, 1:, 1:-1]
        - flux_x[:, 1:-1, :-1, 1:-1]
        + (flux_y[:, 1:-1, 1:-1, 1:] - flux_y[:, 1:-1, 1:-1, :-1])
        + (flux_z[:, 1:, 1:-1, 1:-1] - flux_z[:, :-1, 1:-1, 1:-1])
    )
    hydro_new = interior[:5] - TIME_STEP * change[:5]
    xflux_by = flux_x[6, 1:-1]
    yflux_bx = flux_y[5, 1:-1]
    emf_z = 0.25 * (
        yflux_bx[:, 1:, :] + yflux_bx[:, :-1, :] - (xflux_by[:, :, 1:] + xflux_by[:, :, :-1])
    )
    xflux_bz = flux_x[7, :, :, 1:-1]
    zflux_bx = flux_z[5, :, :, 1:-1]
    emf_y = 0.25 * (xflux_bz[1:] + xflux_bz[:-1] - (zflux_bx[:, 1:] + zflux_bx[:, :-1]))
    yflux_bz = flux_y[7, :, 1:-1, :]
    zflux_by = flux_z[6, :, 1:-1, :]
    emf_x = 0.25 * (zflux_by[:, :, 1:] + zflux_by[:, :, :-1] - (yflux_bz[1:] + yflux_bz[:-1]))
    ez_mid_x = 0.5 * (emf_z[:, 1:] + emf_z[:, :-1])
    ez_mid_y = 0.5 * (emf_z[:, :, 1:] + emf_z[:, :, :-1])
    ey_mid_x = 0.5 * (emf_y[:, 1:] + emf_y[:, :-1])
    ey_mid_z = 0.5 * (emf_y[1:] + emf_y[:-1])
    ex_mid_y = 0.5 * (emf_x[:, :, 1:] + emf_x[:, :, :-1])
    ex_mid_z = 0.5 * (emf_x[1:] + emf_x[:-1])
    field_x = interior[5] - TIME_STEP * (
        ez_mid_x[:, :, 1:] - ez_mid_x[:, :, :-1] - (ey_mid_x[1:] - ey_mid_x[:-1])
    )
    field_y = interior[6] - TIME_STEP * (
        ex_mid_y[1:] - ex_mid_y[:-1] - (ez_mid_y[:, 1:] - ez_mid_y[:, :-1])
    )
    field_z = interior[7] - TIME_STEP * (
        ey_mid_z[:, 1:] - ey_mid_z[:, :-1] - (ex_mid_z[:, :, 1:] - ex_mid_z[:, :, :-1])
    )
    momentum_x = hydro_new[1] + TIME_STEP * 2.0 * ROTATION * interior[2]
    momentum_y = hydro_new[2] + TIME_STEP * (SHEAR_RATE - 2.0) * ROTATION * interior[1]
    return jnp.stack(
        [
            hydro_new[0],
            momentum_x,
            momentum_y,
            hydro_new[3],
            hydro_new[4],
            field_x,
            field_y,
            field_z,
        ]
    )


def window_rows(source, starts, width):
    row_dim = source.ndim - 2

    def pick(row, start):
        return lax.dynamic_slice_in_dim(row, start, width, axis=row.ndim - 1)

    return jax.vmap(pick, in_axes=(row_dim, 0), out_axes=row_dim)(source, starts)


def cycle_window(whole, offsets, block_width, cycle_cells):
    first_column = lax.axis_index("az") * block_width
    starts = jnp.mod(first_column - offsets, cycle_cells)
    wrapped = jnp.concatenate([whole, whole[..., :block_width]], axis=whole.ndim - 1)
    return window_rows(wrapped, starts, block_width)


def roll_rows(wide, offsets):
    cycle_cells = wide.shape[2]
    starts = jnp.mod(cycle_cells - offsets, cycle_cells)
    doubled = jnp.concatenate([wide, wide], axis=2)
    return window_rows(doubled, starts, cycle_cells)


def per_device(state, orbit_shift, remap_shift):
    block_width = state.shape[3]
    azimuth_devices = lax.axis_size("az")
    cycle_cells = block_width * azimuth_devices
    fields, planes, rows = (state.shape[0], state.shape[1], state.shape[2])
    flat = state.reshape(fields * planes, rows, block_width)
    wide = lax.all_to_all(flat, "az", split_axis=0, concat_axis=2, tiled=True)
    rolled = roll_rows(wide, orbit_shift)
    moved = lax.all_to_all(rolled, "az", split_axis=2, concat_axis=0, tiled=True).reshape(
        state.shape
    )
    extended = with_halo(moved, (("rad", 2),), 1)
    radial_index = lax.axis_index("rad")
    radial_devices = lax.axis_size("rad")
    shear_offset = remap_shift[0]
    lower_offset = jnp.where(radial_index == 0, shear_offset, 0)
    upper_offset = jnp.where(
        radial_index == radial_devices - 1, jnp.mod(cycle_cells - shear_offset, cycle_cells), 0
    )
    boundary_offsets = jnp.stack([lower_offset, upper_offset])
    boundary = jnp.concatenate([extended[:, :, :1], extended[:, :, -1:]], axis=2)
    whole_strip = lax.all_gather(boundary, "az", axis=3, tiled=True)
    remapped = cycle_window(whole_strip, boundary_offsets, block_width, cycle_cells)
    extended = jnp.concatenate(
        [remapped[:, :, :1], extended[:, :, 1:-1], remapped[:, :, 1:]], axis=2
    )
    padded = with_halo(extended, (("az", 3), ("vert", 1)), 1)
    return advance(padded)


def solution(mesh):
    return jax.shard_map(
        per_device,
        mesh=mesh,
        in_specs=(P("groups", "vert", "rad", "az"), P(("groups", "rad")), P("groups")),
        out_specs=P("groups", "vert", "rad", "az"),
        check_vma=False,
    )
```

profile of v0, /device:TPU:0, one launch (start us, length us, event | category | flops | bytes accessed | tf_op | source)
XLA Modules:
  0.0 129.6 jit_solution(3632990596651683879)
XLA Ops:
  0.0 6.3 %all-to-all-start = ((f32[32,32,128]{2,1,0:T(8,128)}), f32[32,32,128]{2,1,0:T(8,128)S(1)}, u32[]{:S(2)}, u32[]{:S(2)}) async-start(f32[32,32,128]{2,1,0:T(8,128)} %bitcast.352), calls=%async_computation | async-start | bytes 1048576 | tf_op jit(solution)/shard_map/all_to_all | solution.py:147
  6.3 0.7 fusion.143
  7.0 13.8 %all-to-all-done = f32[32,32,128]{2,1,0:T(8,128)S(1)} async-done(((f32[32,32,128]{2,1,0:T(8,128)}), f32[32,32,128]{2,1,0:T(8,128)S(1)}, u32[]{:S(2)}, u32[]{:S(2)}) %all-to-all-start) | async-done | bytes 524320 | tf_op jit(solution)/shard_map/all_to_all | solution.py:147
  21.0 13.5 %copy.31 = f32[8,32,1024]{0,1,2:T(8,128)} copy(f32[8,32,1024]{2,1,0:T(8,128)S(1)} %pad_maximum_fusion.2) | data formatting | bytes 2097152 | tf_op jit(solution)/shard_map/concatenate | solution.py:137
  34.5 17.3 %gather_fusion = f32[32,8,512]{1,0,2:T(8,128)} fusion(f32[32,8,1024]{1,0,2:T(8,128)} %bitcast.326, s32[32]{0:T(128)S(1)} %fusion.143), kind=kCustom, calls=%fused_computation | custom fusion | bytes 1048960 | tf_op jit(solution)/shard_map/vmap()/gather | solution.py:122
  51.7 5.2 %copy.32 = f32[8,32,512]{1,0,2:T(8,128)S(1)} copy(f32[8,32,512]{0,1,2:T(8,128)} %bitcast.338) | data formatting | bytes 1048576 | tf_op jit(solution)/shard_map/vmap()/transpose | solution.py:124
  56.9 1.6 %reshape.267 = f32[4,1,32768]{2,1,0:T(1,128)} reshape(f32[512,8,32]{2,1,0:T(8,128)S(1)} %bitcast.339) | data formatting | bytes 1048576
  58.5 3.7 %all-to-all-start.1 = ((f32[4,1,32768]{2,1,0:T(1,128)}), f32[4,1,32768]{2,1,0:T(1,128)S(1)}, u32[]{:S(2)}, u32[]{:S(2)}) async-start(f32[4,1,32768]{2,1,0:T(1,128)} %reshape.267), calls=%async_computation.1 | async-start | bytes 1048576 | tf_op jit(solution)/shard_map/all_to_all | solution.py:149
  62.9 13.1 %all-to-all-done.1 = f32[4,1,32768]{2,1,0:T(1,128)S(1)} async-done(((f32[4,1,32768]{2,1,0:T(1,128)}), f32[4,1,32768]{2,1,0:T(1,128)S(1)}, u32[]{:S(2)}, u32[]{:S(2)}) %all-to-all-start.1) | async-done | bytes 524320 | tf_op jit(solution)/shard_map/all_to_all | solution.py:149
  76.5 2.1 %reduce = f32[4,32768]{1,0:T(4,128)S(1)} reduce(f32[4,1,32768]{2,1,0:T(1,128)S(1)} %all-to-all-done.1, f32[]{:T(128)} %broadcast.564), dimensions={1}, to_apply=%all_to_all.28.reduce_sub_computation | reduce | bytes 1048580 | tf_op jit(solution)/shard_map/all_to_all | solution.py:149
  78.6 0.7 reshape.268
  79.4 0.7 copy.44
  80.2 1.6 %collective-permute-start.1 = (f32[8,4,1,128]{3,2,1,0:T(1,128)S(1)}, f32[8,4,1,128]{3,2,1,0:T(1,128)S(1)}, u32[]{:S(2)}, u32[]{:S(2)}) collective-permute-start(f32[8,4,1,128]{3,2,1,0:T(1,128)S(1)} %get-tuple-element.89), channel_id=1, source_target_pairs={{2,0},{0,2},{3,1},{1,3},{6,4},{4,6},{7,5},{5,7},{10,8},{8,10},{11,... | collective-permute-start | bytes 49160 | tf_op jit(solution)/shard_map/ppermute | solution.py:21
  81.7 0.5 collective-permute-start
  82.4 1.6 %collective-permute-done.1 = f32[8,4,1,128]{3,2,1,0:T(1,128)S(1)} collective-permute-done((f32[8,4,1,128]{3,2,1,0:T(1,128)S(1)}, f32[8,4,1,128]{3,2,1,0:T(1,128)S(1)}, u32[]{:S(2)}, u32[]{:S(2)}) %collective-permute-start.1) | collective-permute-done | bytes 16416 | tf_op jit(solution)/shard_map/ppermute | solution.py:21
  84.0 1.5 %collective-permute-done = f32[8,4,1,128]{3,2,1,0:T(1,128)S(1)} collective-permute-done((f32[8,4,1,128]{3,2,1,0:T(1,128)S(1)}, f32[8,4,1,128]{3,2,1,0:T(1,128)S(1)}, u32[]{:S(2)}, u32[]{:S(2)}) %collective-permute-start) | collective-permute-done | bytes 16416 | tf_op jit(solution)/shard_map/ppermute | solution.py:18
  85.5 13.3 %all_gather.3 = f32[8,4,2,512]{3,0,2,1:T(8,128)S(1)} all-gather(f32[8,4,2,128]{3,0,2,1:T(8,128)S(1)} %pad_maximum_fusion.10), channel_id=1, replica_groups=mesh['groups'=2,'az'=4,'rad'=2,'vert'=2] {'az'}, dimensions={3}, use_global_device_ids=true | all-gather | bytes 163840 | tf_op jit(solution)/shard_map/all_gather | solution.py:162
  98.8 1.2 copy.37
  100.0 1.7 %gather_fusion.1 = f32[2,8,4,128]{1,2,3,0:T(4,128)} fusion(f32[2,8,4,640]{1,2,0,3:T(4,128)S(1)} %bitcast.341, s32[2]{0:T(128)S(1)} %fusion.144), kind=kCustom, calls=%fused_computation.1 | custom fusion | bytes 65568 | tf_op jit(solution)/shard_map/vmap()/gather | solution.py:122
  101.7 1.1 fusion.149
  103.7 1.6 %collective-permute-start.3 = (f32[8,4,34,1]{2,0,3,1:T(8,128)S(1)}, f32[8,4,34,1]{2,0,3,1:T(8,128)S(1)}, u32[]{:S(2)}, u32[]{:S(2)}) collective-permute-start(f32[8,4,34,1]{2,0,3,1:T(8,128)S(1)} %copy.41), channel_id=1, source_target_pairs={{4,0},{8,4},{12,8},{0,12},{5,1},{9,5},{13,9},{1,13},{6,2},{10,6},{... | collective-permute-start | bytes 13064 | tf_op jit(solution)/shard_map/ppermute | solution.py:21
  106.1 1.4 %collective-permute-done.3 = f32[8,4,34,1]{2,0,3,1:T(8,128)S(1)} collective-permute-done((f32[8,4,34,1]{2,0,3,1:T(8,128)S(1)}, f32[8,4,34,1]{2,0,3,1:T(8,128)S(1)}, u32[]{:S(2)}, u32[]{:S(2)}) %collective-permute-start.3) | collective-permute-done | bytes 4384 | tf_op jit(solution)/shard_map/ppermute | solution.py:21
  107.8 3.4 %collective-permute-done.2 = f32[8,4,34,1]{2,0,3,1:T(8,128)S(1)} collective-permute-done((f32[8,4,34,1]{2,0,3,1:T(8,128)S(1)}, f32[8,4,34,1]{2,0,3,1:T(8,128)S(1)}, u32[]{:S(2)}, u32[]{:S(2)}) %collective-permute-start.2) | collective-permute-done | bytes 4384 | tf_op jit(solution)/shard_map/ppermute | solution.py:18
  112.5 1.1 collective-permute-done.4
  114.1 0.7 pad_maximum_fusion
  115.0 1.4 %maximum_maximum_fusion = (f32[8,5,34,130]{3,2,1,0:T(8,128)S(1)}, f32[8,5,34,130]{3,2,1,0:T(8,128)S(1)}) fusion(f32[8,4,34,1]{3,2,1,0:T(8,128)S(1)} %copy.43, f32[8,4,1,128]{3,2,1,0:T(1,128)S(1)} %copy.39, f32[8,4,32,128]{3,2,1,0:T(8,128)S(1)} %bitcast.331, f32[8,4,1,128]{3,2,1,0:T(1,128)S(1)} %copy.38, f32[8,4,34,1]{3,2,1,0:T(8,128)S(1)} %copy.42, ...), kind=kLoop, calls=%fused_computation.11 | loop fusion | flops 1768000 | bytes 2263040 | tf_op jit(solution)/shard_map/concatenate | solution.py:22
  119.2 0.6 multiply_reduce_fusion.7
  121.4 0.7 multiply_reduce_fusion.1
  124.5 0.7 fusion.5
  125.2 1.1 fusion.2
  128.1 0.8 copy-done
  128.9 0.7 constant_dynamic-update-slice_fusion
  (95 shorter events, 13.0 us)
Async XLA Ops:
  0.0 20.8 %all-to-all-start = ((f32[32,32,128]{2,1,0:T(8,128)}), f32[32,32,128]{2,1,0:T(8,128)S(1)}, u32[]{:S(2)}, u32[]{:S(2)}) async-start(f32[32,32,128]{2,1,0:T(8,128)} %bitcast.352), calls=%async_computation | async-start | bytes 1048576 | tf_op jit(solution)/shard_map/all_to_all | solution.py:147
  58.5 17.4 %all-to-all-start.1 = ((f32[4,1,32768]{2,1,0:T(1,128)}), f32[4,1,32768]{2,1,0:T(1,128)S(1)}, u32[]{:S(2)}, u32[]{:S(2)}) async-start(f32[4,1,32768]{2,1,0:T(1,128)} %reshape.267), calls=%async_computation.1 | async-start | bytes 1048576 | tf_op jit(solution)/shard_map/all_to_all | solution.py:149
  80.2 3.8 %collective-permute-start.1 = (f32[8,4,1,128]{3,2,1,0:T(1,128)S(1)}, f32[8,4,1,128]{3,2,1,0:T(1,128)S(1)}, u32[]{:S(2)}, u32[]{:S(2)}) collective-permute-start(f32[8,4,1,128]{3,2,1,0:T(1,128)S(1)} %get-tuple-element.89), channel_id=1, source_target_pairs={{2,0},{0,2},{3,1},{1,3},{6,4},{4,6},{7,5},{5,7},{10,8},{8,10},{11,... | collective-permute-start | bytes 49160 | tf_op jit(solution)/shard_map/ppermute | solution.py:21
  81.7 3.7 %collective-permute-start = (f32[8,4,1,128]{3,2,1,0:T(1,128)S(1)}, f32[8,4,1,128]{3,2,1,0:T(1,128)S(1)}, u32[]{:S(2)}, u32[]{:S(2)}) collective-permute-start(f32[8,4,1,128]{3,2,1,0:T(1,128)S(1)} %get-tuple-element.88), channel_id=1, source_target_pairs={{0,2},{2,0},{1,3},{3,1},{4,6},{6,4},{5,7},{7,5},{8,10},{10,8},{9,1... | collective-permute-start | bytes 49160 | tf_op jit(solution)/shard_map/ppermute | solution.py:18
  103.7 3.8 %collective-permute-start.3 = (f32[8,4,34,1]{2,0,3,1:T(8,128)S(1)}, f32[8,4,34,1]{2,0,3,1:T(8,128)S(1)}, u32[]{:S(2)}, u32[]{:S(2)}) collective-permute-start(f32[8,4,34,1]{2,0,3,1:T(8,128)S(1)} %copy.41), channel_id=1, source_target_pairs={{4,0},{8,4},{12,8},{0,12},{5,1},{9,5},{13,9},{1,13},{6,2},{10,6},{... | collective-permute-start | bytes 13064 | tf_op jit(solution)/shard_map/ppermute | solution.py:21
  105.6 5.6 %collective-permute-start.2 = (f32[8,4,34,1]{2,0,3,1:T(8,128)S(1)}, f32[8,4,34,1]{2,0,3,1:T(8,128)S(1)}, u32[]{:S(2)}, u32[]{:S(2)}) collective-permute-start(f32[8,4,34,1]{2,0,3,1:T(8,128)S(1)} %copy.40), channel_id=1, source_target_pairs={{0,4},{4,8},{8,12},{12,0},{1,5},{5,9},{9,13},{13,1},{2,6},{6,10},{... | collective-permute-start | bytes 13064 | tf_op jit(solution)/shard_map/ppermute | solution.py:18
  111.9 1.7 %collective-permute-start.4 = (f32[8,1,34,130]{3,2,1,0:T(8,128)S(1)}, f32[8,1,34,130]{3,2,1,0:T(8,128)S(1)}, u32[]{:S(2)}, u32[]{:S(2)}) collective-permute-start(f32[8,1,34,130]{3,2,1,0:T(8,128)S(1)} %get-tuple-element.76), channel_id=1, source_target_pairs={{0,1},{1,0},{2,3},{3,2},{4,5},{5,4},{6,7},{7,6},{8,9},{9,8},{10,11... | collective-permute-start | bytes 424328 | tf_op jit(solution)/shard_map/ppermute | solution.py:18
  112.0 2.1 %collective-permute-start.5 = (f32[8,1,34,130]{3,2,1,0:T(8,128)S(1)}, f32[8,1,34,130]{3,2,1,0:T(8,128)S(1)}, u32[]{:S(2)}, u32[]{:S(2)}) collective-permute-start(f32[8,1,34,130]{3,2,1,0:T(8,128)S(1)} %get-tuple-element.77), channel_id=1, source_target_pairs={{1,0},{0,1},{3,2},{2,3},{5,4},{4,5},{7,6},{6,7},{9,8},{8,9},{11,10... | collective-permute-start | bytes 424328 | tf_op jit(solution)/shard_map/ppermute | solution.py:21
  128.1 0.8 copy-start
where the time goes:
time: 130 us
  local copies, waits for them, and re-layouts  47.3 us (36%)
  waiting for transfers between devices  36.4 us (28%)
  other arithmetic  16.7 us (13%)
  starting transfers between devices  14.7 us (11%)
  blocking collectives  13.3 us (10%)
    gather x2, local copies, waits for them, and re-layouts, pick(): return lax.dynamic_slice_in_dim(row, start, width, axis=row.ndim - 1)  19 us
    all_to_all x1, waiting for transfers between devices, per_device(): wide = lax.all_to_all(flat, 'az', split_axis=0, concat_axis=2, tiled=True)  13.8 us
    concatenate x1, local copies, waits for them, and re-layouts, roll_rows(): doubled = jnp.concatenate([wide, wide], axis=2)  13.5 us
    all_gather x1, blocking collectives, per_device(): whole_strip = lax.all_gather(boundary, 'az', axis=3, tiled=True)  13.3 us
    all_to_all x1, waiting for transfers between devices, per_device(): lax.all_to_all(rolled, 'az', split_axis=2, concat_axis=0, tiled=True)  13.1 us
    all_to_all x1, starting transfers between devices, per_device(): wide = lax.all_to_all(flat, 'az', split_axis=0, concat_axis=2, tiled=True)  6.32 us
    ppermute x3, waiting for transfers between devices, with_halo(): lax.ppermute(lax.slice_in_dim(block, block.shape[dim] - width, None, axis...  5.98 us
    transpose x1, local copies, waits for them, and re-layouts, window_rows(): jax.vmap(pick, in_axes=(row_dim, 0), out_axes=row_dim)(source, starts)  5.15 us
  transfers between devices with their start and end apart: 8, of which 8 were waited for; matrix products, arithmetic and copies ran while one was open for 1% of the time, Pallas kernels for 0%

commit v1 on v0

v1 whole, which is shorter than its diff:
```python
import functools

import jax
import jax.numpy as jnp
from jax import lax
from jax.experimental import pallas as pl
from jax.experimental.pallas import tpu as pltpu
from jax.sharding import PartitionSpec as P

ADIABATIC = 5.0 / 3.0
TIME_STEP = 0.125
ROTATION = 1.0
SHEAR_RATE = 1.5
MESH = pl.DeviceIdType.MESH
LANES = 128


def lane_index(shape):
    return lax.broadcasted_iota(jnp.int32, shape, len(shape) - 1)


def pair_of_step(step, per, planes):
    if per % planes == 0 and planes == 4:
        fields = per // planes
        return (step % fields) * planes + (3 * (step // fields)) % planes
    return step


def move_kernel(
    count,
    rads,
    state,
    shift,
    main,
    ghost_cols,
    ghost_rows,
    side_cols,
    z_main,
    z_cols,
    z_rows,
    z_side,
    rows,
    turned,
    out_cols,
    out_rows,
    send1,
    recv1,
    send2,
    recv2,
    send3,
    recv3,
    send4,
    recv4,
    own_sem,
):
    fields, planes, height, _ = main.shape
    per = fields * planes // count
    group = lax.axis_index("groups")
    me = lax.axis_index("az")
    rad = lax.axis_index("rad")
    core = lax.axis_index("vert")
    up = (rad + 1) % rads
    down = (rad + rads - 1) % rads

    def device(az, r, v):
        return (group, az, r, v)

    barrier = pltpu.get_barrier_semaphore()
    targets = [device((me + d) % count, rad, core) for d in range(1, count)]
    for d in range(count):
        targets.append(device((me + d) % count, up, core))
        if rads > 2:
            targets.append(device((me + d) % count, down, core))
    targets.append(device(me, rad, 1 - core))
    for target in targets:
        pl.semaphore_signal(barrier, inc=1, device_id=target, device_id_type=MESH)
    pl.semaphore_wait(barrier, len(targets))

    def first(step, d):
        pair = pair_of_step(step, per, planes)
        peer = (me + d) % count
        return pltpu.make_async_remote_copy(
            src_ref=state.at[peer * per + pair],
            dst_ref=rows.at[me, pair],
            send_sem=send1.at[step, d],
            recv_sem=recv1.at[step, d],
            device_id=device(peer, rad, core),
            device_id_type=MESH,
        )

    def second(step, d):
        pair = pair_of_step(step, per, planes)
        peer = (me + d) % count
        whole = me * per + pair
        return pltpu.make_async_remote_copy(
            src_ref=turned.at[peer, pair],
            dst_ref=main.at[whole // planes, whole % planes],
            send_sem=send2.at[step, d],
            recv_sem=recv2.at[step, d],
            device_id=device(peer, rad, core),
            device_id_type=MESH,
        )

    own = pltpu.make_async_copy(state.at[pl.ds(me * per, per)], rows.at[me], own_sem.at[0])
    own.start()

    def start_first(step, carry):
        for d in range(1, count):
            first(step, d).start()
        return carry

    lax.fori_loop(0, per, start_first, 0)
    out_cols[...] = jnp.zeros_like(out_cols)
    own.wait()

    tiles = height // 8
    bits = []
    total = count * LANES
    bit = 0
    while (1 << bit) < total:
        bits.append(bit)
        bit += 1

    def turn(step, carry):
        pair = pair_of_step(step, per, planes)
        for d in range(1, count):
            first(step, d).wait_recv()
        lane8 = lane_index((8, LANES))
        sub8 = lax.broadcasted_iota(jnp.int32, (8, LANES), 0)
        for t in range(tiles + 1):
            amount = shift[pl.ds(8 * t, 8), :]
            if t < tiles:
                blocks = [rows[b, pair, pl.ds(8 * t, 8), :] for b in range(count)]
            else:
                blocks = [
                    jnp.where(
                        sub8 == 7,
                        rows[b, pair, pl.ds(height - 1, 1), :],
                        rows[b, pair, pl.ds(0, 1), :],
                    )
                    for b in range(count)
                ]
            for bit in bits:
                if (1 << bit) < LANES:
                    continue
                q = (1 << bit) // LANES
                flag = ((amount >> bit) & 1) == 1
                blocks = [
                    jnp.where(flag, blocks[(b - q) % count], blocks[b]) for b in range(count)
                ]
            for bit in bits:
                if (1 << bit) >= LANES:
                    continue
                flag = ((amount >> bit) & 1) == 1
                blocks = [
                    jnp.where(flag, pltpu.roll(block, 1 << bit, 1), block) for block in blocks
                ]
            inside = lane8 >= (amount & (LANES - 1))
            out = [
                jnp.where(inside, blocks[b], blocks[(b - 1) % count]) for b in range(count)
            ]
            place = 2 * per * t + 2 * pair
            for b in range(count):
                low = jnp.broadcast_to(out[(b - 1) % count][:, LANES - 1 :], (8, LANES))
                high = jnp.broadcast_to(out[(b + 1) % count][:, :1], (8, LANES))
                out_cols[b] = jnp.where(
                    lane8 == place, low, jnp.where(lane8 == place + 1, high, out_cols[b])
                )
                if t < tiles:
                    turned[b, pair, pl.ds(8 * t, 8), :] = out[b]
                else:
                    out_rows[b, 0, pl.ds(pair, 1), :] = out[b][0:1]
                    out_rows[b, 1, pl.ds(pair, 1), :] = out[b][7:8]
        for d in range(1, count):
            second(step, d).start()
        whole = me * per + pair
        main[whole // planes, whole % planes] = turned[me, pair]
        return carry

    lax.fori_loop(0, per, turn, 0)

    late = []
    for d in range(count):
        peer = (me + d) % count
        if d > 0:
            late.append(
                pltpu.make_async_remote_copy(
                    src_ref=out_cols.at[peer],
                    dst_ref=ghost_cols.at[me],
                    send_sem=send3.at[d],
                    recv_sem=recv3.at[d],
                    device_id=device(peer, rad, core),
                    device_id_type=MESH,
                )
            )
        for side, r in ((0, down), (1, up)):
            slot = count + d * 4 + side * 2
            late.append(
                pltpu.make_async_remote_copy(
                    src_ref=out_rows.at[peer, side],
                    dst_ref=ghost_rows.at[side, me],
                    send_sem=send3.at[slot],
                    recv_sem=recv3.at[slot],
                    device_id=device(peer, r, core),
                    device_id_type=MESH,
                )
            )
            late.append(
                pltpu.make_async_remote_copy(
                    src_ref=out_cols.at[peer],
                    dst_ref=side_cols.at[side, me],
                    send_sem=send3.at[slot + 1],
                    recv_sem=recv3.at[slot + 1],
                    device_id=device(peer, r, core),
                    device_id_type=MESH,
                )
            )
    for copy in late:
        copy.start()
    ghost_cols[me] = out_cols[me]

    def wait_second(step, carry):
        for d in range(1, count):
            second(step, d).wait_recv()
        return carry

    def across(index, source, target):
        return pltpu.make_async_remote_copy(
            src_ref=source,
            dst_ref=target,
            send_sem=send4.at[index],
            recv_sem=recv4.at[index],
            device_id=device(me, rad, 1 - core),
            device_id_type=MESH,
        )

    early = per // 2 if per % planes == 0 and planes == 4 else per
    lax.fori_loop(0, early, wait_second, 0)
    last = [
        across(0, main.at[:, planes - 1], z_main.at[0]),
        across(1, main.at[:, 0], z_main.at[1]),
    ]
    for copy in last:
        copy.start()
    for copy in late:
        copy.wait_recv()
    more = [
        across(2, ghost_cols, z_cols),
        across(3, ghost_rows, z_rows),
        across(4, side_cols, z_side),
    ]
    for copy in more:
        copy.start()
    if early < per:
        lax.fori_loop(early, per, wait_second, 0)
    for copy in last + more:
        copy.wait()

    def finish(step, carry):
        for d in range(1, count):
            first(step, d).wait_send()
            second(step, d).wait_send()
        return carry

    lax.fori_loop(0, per, finish, 0)
    for copy in late:
        copy.wait_send()


def primitives(cells):
    density, mx, my, mz, energy, bx, by, bz = cells
    inverse = 1.0 / density
    velocity = (mx * inverse, my * inverse, mz * inverse)
    magnet_sq = bx * bx + by * by + bz * bz
    kinetic = 0.5 * (mx * velocity[0] + my * velocity[1] + mz * velocity[2])
    pressure = (ADIABATIC - 1.0) * (energy - kinetic - 0.5 * magnet_sq)
    total_pressure = pressure + 0.5 * magnet_sq
    projection = velocity[0] * bx + velocity[1] * by + velocity[2] * bz
    fast_speed = jnp.sqrt((ADIABATIC * pressure + magnet_sq) * inverse)
    return velocity, total_pressure, projection, fast_speed


def one_flux(cells, prims, normal, piece):
    velocity, total_pressure, projection, _ = prims
    speed = velocity[normal]
    field = cells[5 + normal]
    if piece == 0:
        return cells[1 + normal]
    if piece < 4:
        value = cells[piece] * speed - cells[piece + 4] * field
        return value + total_pressure if piece == normal + 1 else value
    if piece == 4:
        return (cells[4] + total_pressure) * speed - field * projection
    return cells[piece] * speed - velocity[piece - 5] * field


def face_flux(left, left_prims, right, right_prims, normal, pieces):
    ls, lc = left_prims[0][normal], left_prims[3]
    rs, rc = right_prims[0][normal], right_prims[3]
    low = jnp.minimum(jnp.minimum(ls - lc, rs - rc), 0.0)
    high = jnp.maximum(jnp.maximum(ls + lc, rs + rc), 0.0)
    inverse = 1.0 / (high - low)
    wl = high * inverse
    wr = low * inverse
    wd = low * wl
    out = []
    for piece in pieces:
        if piece == 5 + normal:
            out.append(wd * (right[piece] - left[piece]))
            continue
        out.append(
            wl * one_flux(left, left_prims, normal, piece)
            - wr * one_flux(right, right_prims, normal, piece)
            + wd * (right[piece] - left[piece])
        )
    return out


def step_kernel(
    count,
    main,
    ghost_cols,
    ghost_rows,
    side_cols,
    z_main,
    z_cols,
    z_rows,
    z_side,
    new,
    pad,
    cols,
    edge,
    fx7,
    fy7,
    fyr7,
    change,
    curl,
    zface,
    gy,
    gx6,
    gz6,
):
    fields, planes, height, _ = main.shape
    per = fields * planes // count
    tiles = height // 8
    tall = height + 8
    lane8 = lane_index((8, LANES))
    sub8 = lax.broadcasted_iota(jnp.int32, (8, LANES), 0)
    lane = lane_index((tall, LANES))
    padded = planes + 2

    for f in range(fields):
        for p in range(padded):
            k = (p - 1) % planes
            owner, slot = divmod(f * planes + k, per)
            if 1 <= p <= planes:
                pad[p, f, pl.ds(0, height)] = main[f, k]
                edge_rows = ghost_rows
            else:
                pad[p, f, pl.ds(0, height)] = z_main[0 if p == 0 else 1, f]
                edge_rows = z_rows
            pad[p, f, pl.ds(height, 8)] = jnp.where(
                sub8 == 7,
                edge_rows[1, owner, pl.ds(slot, 1), :],
                edge_rows[0, owner, pl.ds(slot, 1), :],
            )
        for t in range(tiles + 1):
            tile = jnp.ones((8, LANES), jnp.float32)
            for p in range(padded):
                k = (p - 1) % planes
                owner, slot = divmod(f * planes + k, per)
                inner = 1 <= p <= planes
                if t < tiles:
                    source = (ghost_cols if inner else z_cols)[owner]
                else:
                    both = side_cols if inner else z_side
                    source = jnp.where(sub8 == 7, both[1, owner], both[0, owner])
                moved = pltpu.roll(source, (2 * p - 2 * per * t - 2 * slot) % LANES, 1)
                tile = jnp.where(lane8 // 2 == p, moved, tile)
            cols[f, pl.ds(8 * t, 8)] = tile
        tile = jnp.ones((tall, LANES), jnp.float32)
        for p in range(padded):
            tile = jnp.where(lane // 2 == p, pltpu.roll(pad[p, f], 2 * p + 2, 1), tile)
        edge[f] = tile

    def below(x):
        return pltpu.roll(x, 1, 0)

    def above(x):
        return pltpu.roll(x, tall - 1, 0)

    ghost = [cols[f] for f in range(fields)]
    ghost_prims = primitives(ghost)
    last = [edge[f] for f in range(fields)]
    for piece, value in enumerate(
        face_flux(last, primitives(last), ghost, ghost_prims, 1, range(8))
    ):
        gy[piece] = value
    lower = [below(x) for x in ghost]
    gx6[...] = face_flux(lower, primitives(lower), ghost, ghost_prims, 0, (6,))[0]
    higher = [pltpu.roll(x, LANES - 2, 1) for x in ghost]
    gz6[...] = face_flux(ghost, ghost_prims, higher, primitives(higher), 2, (6,))[0]

    def left_of(x, ghosts, p):
        return jnp.where(lane == 0, pltpu.roll(ghosts, LANES - 2 * p, 1), pltpu.roll(x, 1, 1))

    def right_of(x, ghosts, p):
        return jnp.where(
            lane == LANES - 1,
            pltpu.roll(ghosts, LANES - 2 - 2 * p, 1),
            pltpu.roll(x, LANES - 1, 1),
        )

    def in_plane(p, carry):
        cells = [pad[p, f] for f in range(fields)]
        prims = primitives(cells)
        lower = [below(x) for x in cells]
        flux = face_flux(lower, primitives(lower), cells, prims, 0, range(8))
        fx7[p] = flux[7]
        for f in range(5):
            change[p, f] = (above(flux[f]) - flux[f])[:height]
        x6 = flux[6]
        side = [left_of(cells[f], cols[f], p) for f in range(fields)]
        flux = face_flux(side, primitives(side), cells, prims, 1, range(8))
        fy7[p] = flux[7]
        fyr7[p] = right_of(flux[7], gy[7], p)
        for f in range(5):
            change[p, f] += (right_of(flux[f], gy[f], p) - flux[f])[:height]
        y5 = flux[5]
        y5r = right_of(y5, gy[5], p)
        x6l = left_of(x6, gx6[...], p)
        x6r = right_of(x6, gx6[...], p)
        ez = 0.25 * (y5 + below(y5) - (x6 + x6l))
        ezr = 0.25 * (y5r + below(y5r) - (x6r + x6))
        ez_up = above(ez)
        ezr_up = above(ezr)
        curl[p, 0] = (0.5 * ((ezr_up + ezr) - (ez_up + ez)))[:height]
        curl[p, 1] = (0.5 * ((ezr_up + ez_up) - (ezr + ez)))[:height]
        return carry

    lax.fori_loop(0, padded, in_plane, 0)

    def between(q, carry):
        low = [pad[q, f] for f in range(fields)]
        high = [pad[q + 1, f] for f in range(fields)]
        flux = face_flux(low, primitives(low), high, primitives(high), 2, range(8))
        for f in range(5):
            zface[q, f] = flux[f][:height]
        z5, z6 = flux[5], flux[6]
        ey = 0.25 * (fx7[q + 1] + fx7[q] - (z5 + below(z5)))
        ex = 0.25 * (z6 + left_of(z6, gz6[...], q) - (fy7[q + 1] + fy7[q]))
        exr = 0.25 * (right_of(z6, gz6[...], q) + z6 - (fyr7[q + 1] + fyr7[q]))
        ey_up = above(ey)
        zface[q, 5] = (0.5 * (ey_up + ey))[:height]
        zface[q, 6] = (0.5 * (exr + ex))[:height]
        zface[q, 7] = (0.5 * ((ey_up - ey) - (exr - ex)))[:height]
        return carry

    lax.fori_loop(0, planes + 1, between, 0)

    def combine(k, carry):
        p = k + 1
        old = [pad[p, f, pl.ds(0, height)] for f in range(fields)]
        hydro = [
            old[f] - TIME_STEP * (change[p, f] + (zface[p, f] - zface[k, f])) for f in range(5)
        ]
        new[0, k] = hydro[0]
        new[1, k] = hydro[1] + TIME_STEP * 2.0 * ROTATION * old[2]
        new[2, k] = hydro[2] + TIME_STEP * (SHEAR_RATE - 2.0) * ROTATION * old[1]
        new[3, k] = hydro[3]
        new[4, k] = hydro[4]
        new[5, k] = old[5] - TIME_STEP * (curl[p, 0] - (zface[p, 5] - zface[k, 5]))
        new[6, k] = old[6] - TIME_STEP * ((zface[p, 6] - zface[k, 6]) - curl[p, 1])
        new[7, k] = old[7] - TIME_STEP * (zface[p, 7] + zface[k, 7])
        return carry

    lax.fori_loop(0, planes, combine, 0)


def per_device(state, orbit_shift, remap_shift):
    count = lax.axis_size("az")
    rads = lax.axis_size("rad")
    fields, planes, height, width = state.shape
    total = count * width
    per = fields * planes // count
    rad = lax.axis_index("rad")
    offset = remap_shift[0]
    top = jnp.where(rad == rads - 1, offset, 0)
    bottom = jnp.where(rad == 0, total - offset, 0)
    amounts = jnp.concatenate(
        [
            orbit_shift,
            jnp.broadcast_to((orbit_shift[0] + bottom) % total, (7,)),
            ((orbit_shift[height - 1] + top) % total)[None],
        ]
    )
    shift = jnp.broadcast_to(amounts[:, None], (height + 8, LANES))
    f32 = jnp.float32

    def shaped(*shape):
        return jax.ShapeDtypeStruct(shape, f32)

    vmem = pl.BlockSpec(memory_space=pltpu.VMEM)
    dma = pltpu.SemaphoreType.DMA
    moved = pl.pallas_call(
        functools.partial(move_kernel, count, rads),
        out_shape=[
            shaped(fields, planes, height, LANES),
            shaped(count, 8, LANES),
            shaped(2, count, per, LANES),
            shaped(2, count, 8, LANES),
            shaped(2, fields, height, LANES),
            shaped(count, 8, LANES),
            shaped(2, count, per, LANES),
            shaped(2, count, 8, LANES),
        ],
        in_specs=[vmem] * 2,
        out_specs=[vmem] * 8,
        scratch_shapes=[
            pltpu.VMEM((count, per, height, LANES), f32),
            pltpu.VMEM((count, per, height, LANES), f32),
            pltpu.VMEM((count, 8, LANES), f32),
            pltpu.VMEM((count, 2, per, LANES), f32),
            dma((per, count)),
            dma((per, count)),
            dma((per, count)),
            dma((per, count)),
            dma((5 * count,)),
            dma((5 * count,)),
            dma((5,)),
            dma((5,)),
            dma((1,)),
        ],
        compiler_params=pltpu.CompilerParams(
            collective_id=0, has_side_effects=True, vmem_limit_bytes=24 * 1024 * 1024
        ),
        name="move",
    )(state.reshape(fields * planes, height, width), shift)
    tall = height + 8
    return pl.pallas_call(
        functools.partial(step_kernel, count),
        out_shape=shaped(*state.shape),
        in_specs=[vmem] * 8,
        out_specs=vmem,
        scratch_shapes=[
            pltpu.VMEM((planes + 2, fields, tall, LANES), f32),
            pltpu.VMEM((fields, tall, LANES), f32),
            pltpu.VMEM((fields, tall, LANES), f32),
            pltpu.VMEM((planes + 2, tall, LANES), f32),
            pltpu.VMEM((planes + 2, tall, LANES), f32),
            pltpu.VMEM((planes + 2, tall, LANES), f32),
            pltpu.VMEM((planes + 2, 5, height, LANES), f32),
            pltpu.VMEM((planes + 2, 2, height, LANES), f32),
            pltpu.VMEM((planes + 1, 8, height, LANES), f32),
            pltpu.VMEM((8, tall, LANES), f32),
            pltpu.VMEM((tall, LANES), f32),
            pltpu.VMEM((tall, LANES), f32),
        ],
        compiler_params=pltpu.CompilerParams(vmem_limit_bytes=24 * 1024 * 1024),
        name="step",
    )(*moved)


def solution(mesh):
    return jax.shard_map(
        per_device,
        mesh=mesh,
        in_specs=(P("groups", "vert", "rad", "az"), P(("groups", "rad")), P("groups")),
        out_specs=P("groups", "vert", "rad", "az"),
        check_vma=False,
    )
```

time: 130 us -> 42.9 us (0.33)
  local copies, waits for them, and re-layouts: 47.3 us -> 2.38 us
  Pallas kernels: 0 us -> 38.2 us
  waiting for transfers between devices: 36.4 us -> 0 us
  other arithmetic: 16.7 us -> 0.08 us
  starting transfers between devices: 14.7 us -> 0 us
  blocking collectives: 13.3 us -> 0 us
    pallas_call x0 -> x2, Pallas kernels: none -> 38.2 us  [the longest x1 33.8 us: per_device(): pl.pallas_call(functools.partial(move_kernel, count, rads), out_shape=[sh...]
    all_to_all x2 -> x0, waiting for transfers between devices: 26.9 us -> none  [the longest x1 13.8 us: per_device(): wide = lax.all_to_all(flat, 'az', split_axis=0, concat_axis=2, tiled=True)]
    gather x2 -> x0, local copies, waits for them, and re-layouts: 19 us -> none  [pick(): return lax.dynamic_slice_in_dim(row, start, width, axis=row.ndim - 1)]
    concatenate x2 -> x0, local copies, waits for them, and re-layouts: 14.6 us -> none  [the longest x1 13.5 us: roll_rows(): doubled = jnp.concatenate([wide, wide], axis=2)]
    all_gather x1 -> x0, blocking collectives: 13.3 us -> none  [per_device(): whole_strip = lax.all_gather(boundary, 'az', axis=3, tiled=True)]
    all_to_all x2 -> x0, starting transfers between devices: 9.97 us -> none  [the longest x1 6.32 us: per_device(): wide = lax.all_to_all(flat, 'az', split_axis=0, concat_axis=2, tiled=True)]
    ppermute x6 -> x0, waiting for transfers between devices: 9.43 us -> none  [the longest x3 5.98 us: with_halo(): lax.ppermute(lax.slice_in_dim(block, block.shape[dim] - width, None, axis...]
    transpose x1 -> x0, local copies, waits for them, and re-layouts: 5.15 us -> none  [window_rows(): jax.vmap(pick, in_axes=(row_dim, 0), out_axes=row_dim)(source, starts)]
  transfers between devices with their start and end apart: 8 -> 0, of which waited for: 8 -> 0; matrix products, arithmetic and copies ran while one was open for 1% -> 0% of each run, Pallas kernels for 0% -> 0%
where the time goes in v1:
time: 42.9 us; the launch traced here: 42.7 us
  Pallas kernels  38.2 us (89%)
  local copies, waits for them, and re-layouts  2.38 us (6%)
  between operations  1.98 us (5%)
    pallas_call x1, Pallas kernels, per_device(): pl.pallas_call(functools.partial(move_kernel, count, rads), out_shape=[sh...  33.8 us
    pallas_call x1, Pallas kernels, per_device(): pl.pallas_call(functools.partial(step_kernel, count), out_shape=shaped(*s...  4.48 us
    unnamed x4, local copies, waits for them, and re-layouts  1.69 us

profile of v1, /device:TPU:0, one launch (start us, length us, event | category | flops | bytes accessed | tf_op | source)
XLA Modules:
  0.0 42.7 jit_solution(3749397335323021825)
XLA Ops:
  0.7 0.0 copy-start.1
  0.7 0.6 %copy-done.1 = s32[32]{0:T(128)S(1)} copy-done((s32[32]{0:T(128)S(1)}, s32[32]{0:T(128)}, u32[]{:S(2)}) %copy-start.1) | copy-done | bytes 152
  1.3 0.6 %fusion = (s32[1]{0:T(128)}, s32[1]{0:T(128)}) fusion(s32[32]{0:T(128)S(1)} %copy-done.1), kind=kLoop, calls=%fused_computation.1 | loop fusion | bytes 16 | tf_op jit(solution)/shard_map/slice | solution.py:493
  3.2 0.1 pad_add_fusion
  3.3 0.1 broadcast_in_dim.14.shift
  3.4 0.0 copy-start
  3.4 1.0 %copy-done = f32[8,4,32,128]{3,2,1,0:T(8,128)S(1)} copy-done((f32[8,4,32,128]{3,2,1,0:T(8,128)S(1)}, f32[8,4,32,128]{3,2,1,0:T(8,128)}, u32[]{:S(2)}) %copy-start) | copy-done | bytes 524312
  4.4 33.8 %move.1 = (f32[8,4,32,128]{3,2,1,0:T(8,128)S(1)}, f32[4,8,128]{2,1,0:T(8,128)S(1)}, f32[2,4,8,128]{3,2,1,0:T(8,128)S(1)}, f32[2,4,8,128]{3,2,1,0:T(8,128)S(1)}, ...) custom-call(f32[32,32,128]{2,1,0:T(8,128)S(1)} %bitcast.7, ...), custom_call_target="tpu_custom_call" | custom-call | tf_op jit(solution)/shard_map/move/pallas_call | solution.py:505
  38.2 4.5 %step.1 = f32[8,4,32,128]{3,2,1,0:T(8,128)} custom-call(f32[8,4,32,128]{3,2,1,0:T(8,128)S(1)} %get-tuple-element.13.main, f32[4,8,128]{2,1,0:T(8,128)S(1)} %get-tuple-element.14.ghost_cols, f32[2,4,8,128]{3,2,1,0:T(8,128)S(1)} %get-tuple-element.15.ghost_rows, f32[2,4,8,128]{3,2,1,0:T(8,128)S(1)} %get-tuple-element.16.side_cols, ...), custom_call_target="tpu_custom_call" | custom-call | tf_op jit(solution)/shard_map/step/pallas_call | solution.py:540
  (1 shorter events, 0.0 us)
Async XLA Ops:
  0.7 0.7 %copy-start.1 = (s32[32]{0:T(128)S(1)}, s32[32]{0:T(128)}, u32[]{:S(2)}) copy-start(s32[32]{0:T(128)} %param.4) | copy-start | bytes 388
  3.4 1.0 %copy-start = (f32[8,4,32,128]{3,2,1,0:T(8,128)S(1)}, f32[8,4,32,128]{3,2,1,0:T(8,128)}, u32[]{:S(2)}) copy-start(f32[8,4,32,128]{3,2,1,0:T(8,128)} %param.3) | copy-start | bytes 1572868

commit v2 on v1

--- a/solution.py
+++ b/solution.py
@@ -19,18 +19,29 @@
     return lax.broadcasted_iota(jnp.int32, shape, len(shape) - 1)
 
 
+def halves_of(per, planes):
+    return 2 if per % planes == 0 and planes == 4 else 1
+
+
 def pair_of_step(step, per, planes):
-    if per % planes == 0 and planes == 4:
+    if halves_of(per, planes) == 2:
         fields = per // planes
         return (step % fields) * planes + (3 * (step // fields)) % planes
     return step
 
 
+def place_of_pair(pair, per, planes):
+    held = per // halves_of(per, planes)
+    steps = {pair_of_step(step, per, planes): step for step in range(per)}
+    return divmod(steps[pair], held)
+
+
 def move_kernel(
     count,
     rads,
+    orbit,
+    remap,
     state,
-    shift,
     main,
     ghost_cols,
     ghost_rows,
@@ -41,6 +52,7 @@
     z_side,
     rows,
     turned,
+    shift,
     out_cols,
     out_rows,
     send1,
@@ -55,6 +67,11 @@
 ):
     fields, planes, height, _ = main.shape
     per = fields * planes // count
+    halves = halves_of(per, planes)
+    held = per // halves
+    sides = side_cols.shape[0]
+    total = count * LANES
+    tiles = height // 8
     group = lax.axis_index("groups")
     me = lax.axis_index("az")
     rad = lax.axis_index("rad")
@@ -69,11 +86,26 @@
     targets = [device((me + d) % count, rad, core) for d in range(1, count)]
     for d in range(count):
         targets.append(device((me + d) % count, up, core))
-        if rads > 2:
+        if sides > 1:
             targets.append(device((me + d) % count, down, core))
     targets.append(device(me, rad, 1 - core))
     for target in targets:
         pl.semaphore_signal(barrier, inc=1, device_id=target, device_id_type=MESH)
+
+    own = pltpu.make_async_copy(state.at[pl.ds(me * per, per)], rows.at[me], own_sem.at[0])
+    own.start()
+    lane8 = lane_index((8, LANES))
+    sub8 = lax.broadcasted_iota(jnp.int32, (8, LANES), 0)
+    for t in range(tiles):
+        amount = jnp.full((8, LANES), orbit[8 * t], jnp.int32)
+        for i in range(1, 8):
+            amount = jnp.where(sub8 == i, orbit[8 * t + i], amount)
+        shift[pl.ds(8 * t, 8), :] = amount
+    top = orbit[height - 1] + jnp.where(rad == rads - 1, remap[0], 0)
+    bottom = orbit[0] + jnp.where(rad == 0, total - remap[0], 0)
+    amount = jnp.where(sub8 == 7, top, bottom)
+    shift[pl.ds(height, 8), :] = jnp.where(amount >= total, amount - total, amount)
+    out_cols[...] = jnp.zeros_like(out_cols)
     pl.semaphore_wait(barrier, len(targets))
 
     def first(step, d):
@@ -101,8 +133,32 @@
             device_id_type=MESH,
         )
 
-    own = pltpu.make_async_copy(state.at[pl.ds(me * per, per)], rows.at[me], own_sem.at[0])
-    own.start()
+    def ghosts(half):
+        copies = []
+        base = half * 5 * count
+
+        def add(source, target, slot, d, r):
+            copies.append(
+                pltpu.make_async_remote_copy(
+                    src_ref=source,
+                    dst_ref=target,
+                    send_sem=send3.at[base + slot],
+                    recv_sem=recv3.at[base + slot],
+                    device_id=device((me + d) % count, r, core),
+                    device_id_type=MESH,
+                )
+            )
+
+        for d in range(count):
+            peer = (me + d) % count
+            if d > 0:
+                add(out_cols.at[half, peer], ghost_cols.at[half, me], d, d, rad)
+            for side in range(sides):
+                r = up if side == sides - 1 else down
+                slot = count + d * 4 + side * 2
+                add(out_rows.at[half, peer], ghost_rows.at[side, half, me], slot, d, r)
+                add(out_cols.at[half, peer], side_cols.at[side, half, me], slot + 1, d, r)
+        return copies
 
     def start_first(step, carry):
         for d in range(1, count):
@@ -110,23 +166,14 @@
         return carry
 
     lax.fori_loop(0, per, start_first, 0)
-    out_cols[...] = jnp.zeros_like(out_cols)
     own.wait()
-
-    tiles = height // 8
-    bits = []
-    total = count * LANES
-    bit = 0
-    while (1 << bit) < total:
-        bits.append(bit)
-        bit += 1
-
-    def turn(step, carry):
+    bits = [bit for bit in range(31) if (1 << bit) < total]
+
+    def turn(step, half):
         pair = pair_of_step(step, per, planes)
+        slot = step - half * held
         for d in range(1, count):
             first(step, d).wait_recv()
-        lane8 = lane_index((8, LANES))
-        sub8 = lax.broadcasted_iota(jnp.int32, (8, LANES), 0)
         for t in range(tiles + 1):
             amount = shift[pl.ds(8 * t, 8), :]
             if t < tiles:
@@ -159,65 +206,35 @@
             out = [
                 jnp.where(inside, blocks[b], blocks[(b - 1) % count]) for b in range(count)
             ]
-            place = 2 * per * t + 2 * pair
+            place = 2 * held * t + 2 * slot
             for b in range(count):
                 low = jnp.broadcast_to(out[(b - 1) % count][:, LANES - 1 :], (8, LANES))
                 high = jnp.broadcast_to(out[(b + 1) % count][:, :1], (8, LANES))
-                out_cols[b] = jnp.where(
-                    lane8 == place, low, jnp.where(lane8 == place + 1, high, out_cols[b])
+                out_cols[half, b] = jnp.where(
+                    lane8 == place, low, jnp.where(lane8 == place + 1, high, out_cols[half, b])
                 )
                 if t < tiles:
                     turned[b, pair, pl.ds(8 * t, 8), :] = out[b]
                 else:
-                    out_rows[b, 0, pl.ds(pair, 1), :] = out[b][0:1]
-                    out_rows[b, 1, pl.ds(pair, 1), :] = out[b][7:8]
+                    out_rows[half, b, pl.ds(slot, 1), :] = out[b][0:1]
+                    out_rows[half, b, pl.ds(held + slot, 1), :] = out[b][7:8]
         for d in range(1, count):
             second(step, d).start()
         whole = me * per + pair
         main[whole // planes, whole % planes] = turned[me, pair]
-        return carry
-
-    lax.fori_loop(0, per, turn, 0)
-
-    late = []
-    for d in range(count):
-        peer = (me + d) % count
-        if d > 0:
-            late.append(
-                pltpu.make_async_remote_copy(
-                    src_ref=out_cols.at[peer],
-                    dst_ref=ghost_cols.at[me],
-                    send_sem=send3.at[d],
-                    recv_sem=recv3.at[d],
-                    device_id=device(peer, rad, core),
-                    device_id_type=MESH,
-                )
-            )
-        for side, r in ((0, down), (1, up)):
-            slot = count + d * 4 + side * 2
-            late.append(
-                pltpu.make_async_remote_copy(
-                    src_ref=out_rows.at[peer, side],
-                    dst_ref=ghost_rows.at[side, me],
-                    send_sem=send3.at[slot],
-                    recv_sem=recv3.at[slot],
-                    device_id=device(peer, r, core),
-                    device_id_type=MESH,
-                )
-            )
-            late.append(
-                pltpu.make_async_remote_copy(
-                    src_ref=out_cols.at[peer],
-                    dst_ref=side_cols.at[side, me],
-                    send_sem=send3.at[slot + 1],
-                    recv_sem=recv3.at[slot + 1],
-                    device_id=device(peer, r, core),
-                    device_id_type=MESH,
-                )
-            )
-    for copy in late:
-        copy.start()
-    ghost_cols[me] = out_cols[me]
+
+    small = []
+    for half in range(halves):
+
+        def body(step, carry, half=half):
+            turn(step, half)
+            return carry
+
+        lax.fori_loop(half * held, (half + 1) * held, body, 0)
+        small.append(ghosts(half))
+        for copy in small[half]:
+            copy.start()
+        ghost_cols[half, me] = out_cols[half, me]
 
     def wait_second(step, carry):
         for d in range(1, count):
@@ -234,26 +251,24 @@
             device_id_type=MESH,
         )
 
-    early = per // 2 if per % planes == 0 and planes == 4 else per
-    lax.fori_loop(0, early, wait_second, 0)
+    lax.fori_loop(0, held, wait_second, 0)
+    for copy in small[0]:
+        copy.wait_recv()
     last = [
         across(0, main.at[:, planes - 1], z_main.at[0]),
         across(1, main.at[:, 0], z_main.at[1]),
+        across(2, ghost_cols.at[0], z_cols),
     ]
+    for side in range(sides):
+        last.append(across(3 + 2 * side, ghost_rows.at[side, 0], z_rows.at[side]))
+        last.append(across(4 + 2 * side, side_cols.at[side, 0], z_side.at[side]))
     for copy in last:
         copy.start()
-    for copy in late:
-        copy.wait_recv()
-    more = [
-        across(2, ghost_cols, z_cols),
-        across(3, ghost_rows, z_rows),
-        across(4, side_cols, z_side),
-    ]
-    for copy in more:
-        copy.start()
-    if early < per:
-        lax.fori_loop(early, per, wait_second, 0)
-    for copy in last + more:
+    for half in range(1, halves):
+        lax.fori_loop(half * held, (half + 1) * held, wait_second, 0)
+        for copy in small[half]:
+            copy.wait_recv()
+    for copy in last:
         copy.wait()
 
     def finish(step, carry):
@@ -263,8 +278,9 @@
         return carry
 
     lax.fori_loop(0, per, finish, 0)
-    for copy in late:
-        copy.wait_send()
+    for half in range(halves):
+        for copy in small[half]:
+            copy.wait_send()
 
 
 def primitives(cells):
@@ -326,7 +342,9 @@
     z_cols,
     z_rows,
     z_side,
+    result,
     new,
+    sems,
     pad,
     cols,
     edge,
@@ -349,33 +367,42 @@
     lane = lane_index((tall, LANES))
     padded = planes + 2
 
+    sides = side_cols.shape[0]
+    held = per // halves_of(per, planes)
+
+    def source_of(f, p):
+        k = (p - 1) % planes
+        owner, pair = divmod(f * planes + k, per)
+        half, slot = place_of_pair(pair, per, planes)
+        return k, owner, half, slot
+
     for f in range(fields):
         for p in range(padded):
-            k = (p - 1) % planes
-            owner, slot = divmod(f * planes + k, per)
+            k, owner, half, slot = source_of(f, p)
+            low, high = pl.ds(slot, 1), pl.ds(held + slot, 1)
             if 1 <= p <= planes:
                 pad[p, f, pl.ds(0, height)] = main[f, k]
-                edge_rows = ghost_rows
+                before = ghost_rows[sides - 1, half, owner, high, :]
+                after = ghost_rows[0, half, owner, low, :]
             else:
                 pad[p, f, pl.ds(0, height)] = z_main[0 if p == 0 else 1, f]
-                edge_rows = z_rows
-            pad[p, f, pl.ds(height, 8)] = jnp.where(
-                sub8 == 7,
-                edge_rows[1, owner, pl.ds(slot, 1), :],
-                edge_rows[0, owner, pl.ds(slot, 1), :],
-            )
+                before = z_rows[sides - 1, owner, high, :]
+                after = z_rows[0, owner, low, :]
+            pad[p, f, pl.ds(height, 8)] = jnp.where(sub8 == 7, before, after)
         for t in range(tiles + 1):
             tile = jnp.ones((8, LANES), jnp.float32)
             for p in range(padded):
-                k = (p - 1) % planes
-                owner, slot = divmod(f * planes + k, per)
+                k, owner, half, slot = source_of(f, p)
                 inner = 1 <= p <= planes
                 if t < tiles:
-                    source = (ghost_cols if inner else z_cols)[owner]
+                    source = ghost_cols[half, owner] if inner else z_cols[owner]
+                elif inner:
+                    source = jnp.where(
+                        sub8 == 7, side_cols[sides - 1, half, owner], side_cols[0, half, owner]
+                    )
                 else:
-                    both = side_cols if inner else z_side
-                    source = jnp.where(sub8 == 7, both[1, owner], both[0, owner])
-                moved = pltpu.roll(source, (2 * p - 2 * per * t - 2 * slot) % LANES, 1)
+                    source = jnp.where(sub8 == 7, z_side[sides - 1, owner], z_side[0, owner])
+                moved = pltpu.roll(source, (2 * p - 2 * held * t - 2 * slot) % LANES, 1)
                 tile = jnp.where(lane8 // 2 == p, moved, tile)
             cols[f, pl.ds(8 * t, 8)] = tile
         tile = jnp.ones((tall, LANES), jnp.float32)
@@ -472,77 +499,78 @@
         new[5, k] = old[5] - TIME_STEP * (curl[p, 0] - (zface[p, 5] - zface[k, 5]))
         new[6, k] = old[6] - TIME_STEP * ((zface[p, 6] - zface[k, 6]) - curl[p, 1])
         new[7, k] = old[7] - TIME_STEP * (zface[p, 7] + zface[k, 7])
+        store(k).start()
         return carry
 
+    def store(k):
+        return pltpu.make_async_copy(new.at[:, k], result.at[:, k], sems.at[k])
+
     lax.fori_loop(0, planes, combine, 0)
+    for k in range(planes):
+        store(k).wait()
 
 
 def per_device(state, orbit_shift, remap_shift):
     count = lax.axis_size("az")
     rads = lax.axis_size("rad")
     fields, planes, height, width = state.shape
-    total = count * width
     per = fields * planes // count
-    rad = lax.axis_index("rad")
-    offset = remap_shift[0]
-    top = jnp.where(rad == rads - 1, offset, 0)
-    bottom = jnp.where(rad == 0, total - offset, 0)
-    amounts = jnp.concatenate(
-        [
-            orbit_shift,
-            jnp.broadcast_to((orbit_shift[0] + bottom) % total, (7,)),
-            ((orbit_shift[height - 1] + top) % total)[None],
-        ]
-    )
-    shift = jnp.broadcast_to(amounts[:, None], (height + 8, LANES))
+    halves = halves_of(per, planes)
+    held = per // halves
+    sides = 1 if rads == 2 else 2
     f32 = jnp.float32
 
     def shaped(*shape):
         return jax.ShapeDtypeStruct(shape, f32)
 
     vmem = pl.BlockSpec(memory_space=pltpu.VMEM)
+    smem = pl.BlockSpec(memory_space=pltpu.SMEM)
+    anywhere = pl.BlockSpec(memory_space=pl.ANY)
     dma = pltpu.SemaphoreType.DMA
     moved = pl.pallas_call(
         functools.partial(move_kernel, count, rads),
         out_shape=[
             shaped(fields, planes, height, LANES),
-            shaped(count, 8, LANES),
-            shaped(2, count, per, LANES),
-            shaped(2, count, 8, LANES),
+            shaped(halves, count, 8, LANES),
+            shaped(sides, halves, count, 2 * held, LANES),
+            shaped(sides, halves, count, 8, LANES),
             shaped(2, fields, height, LANES),
             shaped(count, 8, LANES),
-            shaped(2, count, per, LANES),
-            shaped(2, count, 8, LANES),
+            shaped(sides, count, 2 * held, LANES),
+            shaped(sides, count, 8, LANES),
         ],
-        in_specs=[vmem] * 2,
+        in_specs=[smem, smem, anywhere],
         out_specs=[vmem] * 8,
         scratch_shapes=[
             pltpu.VMEM((count, per, height, LANES), f32),
             pltpu.VMEM((count, per, height, LANES), f32),
-            pltpu.VMEM((count, 8, LANES), f32),
-            pltpu.VMEM((count, 2, per, LANES), f32),
+            pltpu.VMEM((height + 8, LANES), jnp.int32),
+            pltpu.VMEM((halves, count, 8, LANES), f32),
+            pltpu.VMEM((halves, count, 2 * held, LANES), f32),
             dma((per, count)),
             dma((per, count)),
             dma((per, count)),
             dma((per, count)),
-            dma((5 * count,)),
-            dma((5 * count,)),
-            dma((5,)),
-            dma((5,)),
+            dma((5 * count * halves,)),
+            dma((5 * count * halves,)),
+            dma((7,)),
+            dma((7,)),
             dma((1,)),
         ],
         compiler_params=pltpu.CompilerParams(
             collective_id=0, has_side_effects=True, vmem_limit_bytes=24 * 1024 * 1024
         ),
         name="move",
-    )(state.reshape(fields * planes, height, width), shift)
+    )(orbit_shift, remap_shift, state.reshape(fields * planes, height, width))
     tall = height + 8
     return pl.pallas_call(
         functools.partial(step_kernel, count),
         out_shape=shaped(*state.shape),
         in_specs=[vmem] * 8,
-        out_specs=vmem,
+        out_specs=anywhere,
         scratch_shapes=[
+            pltpu.VMEM(state.shape, f32),
+            dma((planes,)),
             pltpu.VMEM((planes + 2, fields, tall, LANES), f32),
             pltpu.VMEM((fields, tall, LANES), f32),
             pltpu.VMEM((fields, tall, LANES), f32),

time: 42.9 us -> 41.2 us (0.960)
  between operations: 1.98 us -> 0.67 us
  local copies, waits for them, and re-layouts: 2.38 us -> 1.69 us
    slice x1 -> x0, local copies, waits for them, and re-layouts: 0.61 us -> none  [per_device(): orbit_shift[0] + bottom]
where the time goes in v2:
time: 41.2 us; the launch traced here: 41 us
  Pallas kernels  38.6 us (94%)
  local copies, waits for them, and re-layouts  1.69 us (4%)
  between operations  0.67 us (2%)
    pallas_call x1, Pallas kernels, per_device(): pl.pallas_call(functools.partial(move_kernel, count, rads), out_shape=[sh...  34.1 us
    pallas_call x1, Pallas kernels, per_device(): pl.pallas_call(functools.partial(step_kernel, count), out_shape=shaped(*s...  4.5 us
    unnamed x4, local copies, waits for them, and re-layouts  1.69 us

profile of v2, /device:TPU:0, one launch (start us, length us, event | category | flops | bytes accessed | tf_op | source)
XLA Modules:
  0.0 41.0 jit_solution(2956963088205792133)
XLA Ops:
  0.7 0.0 copy-start.1
  0.7 0.6 %copy-done.1 = s32[32]{0:T(128)S(1)} copy-done((s32[32]{0:T(128)S(1)}, s32[32]{0:T(128)}, u32[]{:S(2)}) %copy-start.1) | copy-done | bytes 152
  1.3 0.0 copy-start
  1.3 1.0 %copy-done = f32[8,4,32,128]{3,2,1,0:T(8,128)S(1)} copy-done((f32[8,4,32,128]{3,2,1,0:T(8,128)S(1)}, f32[8,4,32,128]{3,2,1,0:T(8,128)}, u32[]{:S(2)}) %copy-start) | copy-done | bytes 524312
  2.4 34.1 %move.1 = (f32[8,4,32,128]{3,2,1,0:T(8,128)S(1)}, f32[2,4,8,128]{3,2,1,0:T(8,128)S(1)}, f32[1,2,4,8,128]{4,3,2,1,0:T(8,128)S(1)}, f32[1,2,4,8,128]{4,3,2,1,0:T(8...) custom-call(s32[32]{0:T(128)S(1)} %copy-done.1, ...), custom_call_target="tpu_custom_call" | custom-call | tf_op jit(solution)/shard_map/move/pallas_call | solution.py:530
  36.5 4.5 %step.1 = f32[8,4,32,128]{3,2,1,0:T(8,128)} custom-call(f32[8,4,32,128]{3,2,1,0:T(8,128)S(1)} %get-tuple-element.13.main, f32[2,4,8,128]{3,2,1,0:T(8,128)S(1)} %get-tuple-element.14.ghost_cols, f32[1,2,4,8,128]{4,3,2,1,0:T(8,128)S(1)} %get-tuple-element.15.ghost_rows, f32[1,2,4,8,128]{4,3,2,1,0:T(8,128)S(1)} %get-tuple-element.16.side_cols, ...), custom_call_target="tpu_custom_call" | custom-call | tf_op jit(solution)/shard_map/step/pallas_call | solution.py:566
Async XLA Ops:
  0.7 0.7 %copy-start.1 = (s32[32]{0:T(128)S(1)}, s32[32]{0:T(128)}, u32[]{:S(2)}) copy-start(s32[32]{0:T(128)} %orbit.1) | copy-start | bytes 388
  1.3 1.0 %copy-start = (f32[8,4,32,128]{3,2,1,0:T(8,128)S(1)}, f32[8,4,32,128]{3,2,1,0:T(8,128)}, u32[]{:S(2)}) copy-start(f32[8,4,32,128]{3,2,1,0:T(8,128)} %param.3) | copy-start | bytes 1572868

commit v3 on v2

--- a/solution.py
+++ b/solution.py
@@ -39,6 +39,7 @@
 def move_kernel(
     count,
     rads,
+    stages,
     orbit,
     remap,
     state,
@@ -264,12 +265,17 @@
         last.append(across(4 + 2 * side, side_cols.at[side, 0], z_side.at[side]))
     for copy in last:
         copy.start()
+    stages[0]()
+    for copy in last:
+        copy.wait_recv()
+    stages[1]()
     for half in range(1, halves):
         lax.fori_loop(half * held, (half + 1) * held, wait_second, 0)
         for copy in small[half]:
             copy.wait_recv()
+    stages[2]()
     for copy in last:
-        copy.wait()
+        copy.wait_send()
 
     def finish(step, carry):
         for d in range(1, count):
@@ -332,7 +338,7 @@
     return out
 
 
-def step_kernel(
+def step_stages(
     count,
     main,
     ghost_cols,
@@ -342,9 +348,7 @@
     z_cols,
     z_rows,
     z_side,
-    result,
     new,
-    sems,
     pad,
     cols,
     edge,
@@ -376,57 +380,58 @@
         half, slot = place_of_pair(pair, per, planes)
         return k, owner, half, slot
 
-    for f in range(fields):
-        for p in range(padded):
-            k, owner, half, slot = source_of(f, p)
-            low, high = pl.ds(slot, 1), pl.ds(held + slot, 1)
-            if 1 <= p <= planes:
-                pad[p, f, pl.ds(0, height)] = main[f, k]
-                before = ghost_rows[sides - 1, half, owner, high, :]
-                after = ghost_rows[0, half, owner, low, :]
-            else:
-                pad[p, f, pl.ds(0, height)] = z_main[0 if p == 0 else 1, f]
-                before = z_rows[sides - 1, owner, high, :]
-                after = z_rows[0, owner, low, :]
-            pad[p, f, pl.ds(height, 8)] = jnp.where(sub8 == 7, before, after)
-        for t in range(tiles + 1):
-            tile = jnp.ones((8, LANES), jnp.float32)
-            for p in range(padded):
-                k, owner, half, slot = source_of(f, p)
-                inner = 1 <= p <= planes
-                if t < tiles:
-                    source = ghost_cols[half, owner] if inner else z_cols[owner]
-                elif inner:
-                    source = jnp.where(
-                        sub8 == 7, side_cols[sides - 1, half, owner], side_cols[0, half, owner]
-                    )
-                else:
-                    source = jnp.where(sub8 == 7, z_side[sides - 1, owner], z_side[0, owner])
-                moved = pltpu.roll(source, (2 * p - 2 * held * t - 2 * slot) % LANES, 1)
-                tile = jnp.where(lane8 // 2 == p, moved, tile)
-            cols[f, pl.ds(8 * t, 8)] = tile
-        tile = jnp.ones((tall, LANES), jnp.float32)
-        for p in range(padded):
-            tile = jnp.where(lane // 2 == p, pltpu.roll(pad[p, f], 2 * p + 2, 1), tile)
-        edge[f] = tile
-
     def below(x):
         return pltpu.roll(x, 1, 0)
 
     def above(x):
         return pltpu.roll(x, tall - 1, 0)
 
-    ghost = [cols[f] for f in range(fields)]
-    ghost_prims = primitives(ghost)
-    last = [edge[f] for f in range(fields)]
-    for piece, value in enumerate(
-        face_flux(last, primitives(last), ghost, ghost_prims, 1, range(8))
-    ):
-        gy[piece] = value
-    lower = [below(x) for x in ghost]
-    gx6[...] = face_flux(lower, primitives(lower), ghost, ghost_prims, 0, (6,))[0]
-    higher = [pltpu.roll(x, LANES - 2, 1) for x in ghost]
-    gz6[...] = face_flux(ghost, ghost_prims, higher, primitives(higher), 2, (6,))[0]
+    def assemble(chosen, fresh):
+        for f in range(fields):
+            for p in chosen:
+                k, owner, half, slot = source_of(f, p)
+                low, high = pl.ds(slot, 1), pl.ds(held + slot, 1)
+                if 1 <= p <= planes:
+                    pad[p, f, pl.ds(0, height)] = main[f, k]
+                    before = ghost_rows[sides - 1, half, owner, high, :]
+                    after = ghost_rows[0, half, owner, low, :]
+                else:
+                    pad[p, f, pl.ds(0, height)] = z_main[0 if p == 0 else 1, f]
+                    before = z_rows[sides - 1, owner, high, :]
+                    after = z_rows[0, owner, low, :]
+                pad[p, f, pl.ds(height, 8)] = jnp.where(sub8 == 7, before, after)
+            for t in range(tiles + 1):
+                tile = jnp.zeros((8, LANES), jnp.float32) if fresh else cols[f, pl.ds(8 * t, 8)]
+                for p in chosen:
+                    k, owner, half, slot = source_of(f, p)
+                    inner = 1 <= p <= planes
+                    if t < tiles:
+                        source = ghost_cols[half, owner] if inner else z_cols[owner]
+                    elif inner:
+                        source = jnp.where(
+                            sub8 == 7, side_cols[sides - 1, half, owner], side_cols[0, half, owner]
+                        )
+                    else:
+                        source = jnp.where(sub8 == 7, z_side[sides - 1, owner], z_side[0, owner])
+                    moved = pltpu.roll(source, (2 * p - 2 * held * t - 2 * slot) % LANES, 1)
+                    tile = jnp.where(lane8 // 2 == p, moved, tile)
+                cols[f, pl.ds(8 * t, 8)] = tile
+            tile = jnp.zeros((tall, LANES), jnp.float32) if fresh else edge[f]
+            for p in chosen:
+                tile = jnp.where(lane // 2 == p, pltpu.roll(pad[p, f], 2 * p + 2, 1), tile)
+            edge[f] = tile
+
+        ghost = [cols[f] for f in range(fields)]
+        ghost_prims = primitives(ghost)
+        last = [edge[f] for f in range(fields)]
+        for piece, value in enumerate(
+            face_flux(last, primitives(last), ghost, ghost_prims, 1, range(8))
+        ):
+            gy[piece] = value
+        lower = [below(x) for x in ghost]
+        gx6[...] = face_flux(lower, primitives(lower), ghost, ghost_prims, 0, (6,))[0]
+        higher = [pltpu.roll(x, LANES - 2, 1) for x in ghost]
+        gz6[...] = face_flux(ghost, ghost_prims, higher, primitives(higher), 2, (6,))[0]
 
     def left_of(x, ghosts, p):
         return jnp.where(lane == 0, pltpu.roll(ghosts, LANES - 2 * p, 1), pltpu.roll(x, 1, 1))
@@ -465,8 +470,6 @@
         curl[p, 1] = (0.5 * ((ezr_up + ez_up) - (ezr + ez)))[:height]
         return carry
 
-    lax.fori_loop(0, padded, in_plane, 0)
-
     def between(q, carry):
         low = [pad[q, f] for f in range(fields)]
         high = [pad[q + 1, f] for f in range(fields)]
@@ -483,8 +486,6 @@
         zface[q, 7] = (0.5 * ((ey_up - ey) - (exr - ex)))[:height]
         return carry
 
-    lax.fori_loop(0, planes + 1, between, 0)
-
     def combine(k, carry):
         p = k + 1
         old = [pad[p, f, pl.ds(0, height)] for f in range(fields)]
@@ -499,15 +500,42 @@
         new[5, k] = old[5] - TIME_STEP * (curl[p, 0] - (zface[p, 5] - zface[k, 5]))
         new[6, k] = old[6] - TIME_STEP * ((zface[p, 6] - zface[k, 6]) - curl[p, 1])
         new[7, k] = old[7] - TIME_STEP * (zface[p, 7] + zface[k, 7])
-        store(k).start()
         return carry
 
-    def store(k):
-        return pltpu.make_async_copy(new.at[:, k], result.at[:, k], sems.at[k])
-
-    lax.fori_loop(0, planes, combine, 0)
-    for k in range(planes):
-        store(k).wait()
+    def run(body, first, stride, times):
+        lax.fori_loop(0, times, lambda i, carry: body(first + stride * i, carry), 0)
+
+    early = halves_of(per, planes) == 2
+
+    def outer():
+        if early:
+            assemble((1, planes), True)
+            run(in_plane, 1, planes - 1, 2)
+
+    def other_core():
+        assemble((0, planes + 1), not early)
+        run(in_plane, 0, planes + 1, 2)
+        if early:
+            run(between, 0, planes, 2)
+
+    def inner():
+        if early:
+            assemble(tuple(range(2, planes)), False)
+            run(in_plane, 2, 1, planes - 2)
+            run(between, 1, 1, planes - 1)
+        else:
+            assemble(tuple(range(1, planes + 1)), False)
+            run(in_plane, 1, 1, planes)
+            run(between, 0, 1, planes + 1)
+        run(combine, 0, 1, planes)
+
+    return outer, other_core, inner
+
+
+def whole_kernel(count, rads, orbit, remap, state, new, *scratch):
+    landed, rest, work = scratch[:8], scratch[8:22], scratch[22:]
+    stages = step_stages(count, *landed, new, *work)
+    move_kernel(count, rads, stages, orbit, remap, state, *landed, *rest)
 
 
 def per_device(state, orbit_shift, remap_shift):
@@ -520,33 +548,35 @@
     sides = 1 if rads == 2 else 2
     f32 = jnp.float32
 
-    def shaped(*shape):
-        return jax.ShapeDtypeStruct(shape, f32)
-
-    vmem = pl.BlockSpec(memory_space=pltpu.VMEM)
-    smem = pl.BlockSpec(memory_space=pltpu.SMEM)
-    anywhere = pl.BlockSpec(memory_space=pl.ANY)
     dma = pltpu.SemaphoreType.DMA
-    moved = pl.pallas_call(
-        functools.partial(move_kernel, count, rads),
-        out_shape=[
-            shaped(fields, planes, height, LANES),
-            shaped(halves, count, 8, LANES),
-            shaped(sides, halves, count, 2 * held, LANES),
-            shaped(sides, halves, count, 8, LANES),
-            shaped(2, fields, height, LANES),
-            shaped(count, 8, LANES),
-            shaped(sides, count, 2 * held, LANES),
-            shaped(sides, count, 8, LANES),
+    tall = height + 8
+
+    def held_in(*shape):
+        return pltpu.VMEM(shape, f32)
+
+    return pl.pallas_call(
+        functools.partial(whole_kernel, count, rads),
+        out_shape=jax.ShapeDtypeStruct(state.shape, f32),
+        in_specs=[
+            pl.BlockSpec(memory_space=pltpu.SMEM),
+            pl.BlockSpec(memory_space=pltpu.SMEM),
+            pl.BlockSpec(memory_space=pl.ANY),
         ],
-        in_specs=[smem, smem, anywhere],
-        out_specs=[vmem] * 8,
+        out_specs=pl.BlockSpec(memory_space=pltpu.VMEM),
         scratch_shapes=[
-            pltpu.VMEM((count, per, height, LANES), f32),
-            pltpu.VMEM((count, per, height, LANES), f32),
-            pltpu.VMEM((height + 8, LANES), jnp.int32),
-            pltpu.VMEM((halves, count, 8, LANES), f32),
-            pltpu.VMEM((halves, count, 2 * held, LANES), f32),
+            held_in(fields, planes, height, LANES),
+            held_in(halves, count, 8, LANES),
+            held_in(sides, halves, count, 2 * held, LANES),
+            held_in(sides, halves, count, 8, LANES),
+            held_in(2, fields, height, LANES),
+            held_in(count, 8, LANES),
+            held_in(sides, count, 2 * held, LANES),
+            held_in(sides, count, 8, LANES),
+            held_in(count, per, height, LANES),
+            held_in(count, per, height, LANES),
+            pltpu.VMEM((tall, LANES), jnp.int32),
+            held_in(halves, count, 8, LANES),
+            held_in(halves, count, 2 * held, LANES),
             dma((per, count)),
             dma((per, count)),
             dma((per, count)),
@@ -556,37 +586,24 @@
             dma((7,)),
             dma((7,)),
             dma((1,)),
+            held_in(planes + 2, fields, tall, LANES),
+            held_in(fields, tall, LANES),
+            held_in(fields, tall, LANES),
+            held_in(planes + 2, tall, LANES),
+            held_in(planes + 2, tall, LANES),
+            held_in(planes + 2, tall, LANES),
+            held_in(planes + 2, 5, height, LANES),
+            held_in(planes + 2, 2, height, LANES),
+            held_in(planes + 1, 8, height, LANES),
+            held_in(8, tall, LANES),
+            held_in(tall, LANES),
+            held_in(tall, LANES),
         ],
         compiler_params=pltpu.CompilerParams(
             collective_id=0, has_side_effects=True, vmem_limit_bytes=24 * 1024 * 1024
         ),
-        name="move",
+        name="whole",
     )(orbit_shift, remap_shift, state.reshape(fields * planes, height, width))
-    tall = height + 8
-    return pl.pallas_call(
-        functools.partial(step_kernel, count),
-        out_shape=shaped(*state.shape),
-        in_specs=[vmem] * 8,
-        out_specs=anywhere,
-        scratch_shapes=[
-            pltpu.VMEM(state.shape, f32),
-            dma((planes,)),
-            pltpu.VMEM((planes + 2, fields, tall, LANES), f32),
-            pltpu.VMEM((fields, tall, LANES), f32),
-            pltpu.VMEM((fields, tall, LANES), f32),
-            pltpu.VMEM((planes + 2, tall, LANES), f32),
-            pltpu.VMEM((planes + 2, tall, LANES), f32),
-            pltpu.VMEM((planes + 2, tall, LANES), f32),
-            pltpu.VMEM((planes + 2, 5, height, LANES), f32),
-            pltpu.VMEM((planes + 2, 2, height, LANES), f32),
-            pltpu.VMEM((planes + 1, 8, height, LANES), f32),
-            pltpu.VMEM((8, tall, LANES), f32),
-            pltpu.VMEM((tall, LANES), f32),
-            pltpu.VMEM((tall, LANES), f32),
-        ],
-        compiler_params=pltpu.CompilerParams(vmem_limit_bytes=24 * 1024 * 1024),
-        name="step",
-    )(*moved)
 
 
 def solution(mesh):

time: 41.2 us -> 39.2 us (0.951)
  Pallas kernels: 38.6 us -> 35.9 us
  local copies, waits for them, and re-layouts: 1.69 us -> 2.49 us
    pallas_call x2 -> x1, Pallas kernels: 38.6 us -> 35.9 us  [per_device(): pl.pallas_call(functools.partial(whole_kernel, count, rads), out_shape=ja...]
    unnamed x4 -> x5, local copies, waits for them, and re-layouts: 1.69 us -> 2.49 us
where the time goes in v3:
time: 39.2 us; the launch traced here: 39.1 us
  Pallas kernels  35.9 us (92%)
  local copies, waits for them, and re-layouts  2.49 us (6%)
  between operations  0.67 us (2%)
    pallas_call x1, Pallas kernels, per_device(): pl.pallas_call(functools.partial(whole_kernel, count, rads), out_shape=ja...  35.9 us
    unnamed x5, local copies, waits for them, and re-layouts  2.49 us

profile of v3, /device:TPU:0, one launch (start us, length us, event | category | flops | bytes accessed | tf_op | source)
XLA Modules:
  0.0 39.1 jit_solution(18089295335312664596)
XLA Ops:
  0.7 0.0 copy-start.1
  0.7 0.6 %copy-done.1 = s32[32]{0:T(128)S(1)} copy-done((s32[32]{0:T(128)S(1)}, s32[32]{0:T(128)}, u32[]{:S(2)}) %copy-start.1) | copy-done | bytes 152
  1.3 0.0 copy-start
  1.3 1.0 %copy-done = f32[8,4,32,128]{3,2,1,0:T(8,128)S(1)} copy-done((f32[8,4,32,128]{3,2,1,0:T(8,128)S(1)}, f32[8,4,32,128]{3,2,1,0:T(8,128)}, u32[]{:S(2)}) %copy-start) | copy-done | bytes 524312
  2.4 35.9 %whole.1 = f32[8,4,32,128]{3,2,1,0:T(8,128)S(1)} custom-call(s32[32]{0:T(128)S(1)} %copy-done.1, s32[1]{0:T(128)S(6)} %copy.5.remap, f32[32,32,128]{2,1,0:T(8,128)S(1)} %bitcast.1), custom_call_target="tpu_custom_call" | custom-call | tf_op jit(solution)/shard_map/whole/pallas_call | solution.py:557
  38.3 0.8 %copy.6 = f32[8,4,32,128]{3,2,1,0:T(8,128)} copy(f32[8,4,32,128]{3,2,1,0:T(8,128)S(1)} %whole.1) | data formatting | bytes 1048576
Async XLA Ops:
  0.7 0.7 %copy-start.1 = (s32[32]{0:T(128)S(1)}, s32[32]{0:T(128)}, u32[]{:S(2)}) copy-start(s32[32]{0:T(128)} %orbit.1) | copy-start | bytes 388
  1.3 1.0 %copy-start = (f32[8,4,32,128]{3,2,1,0:T(8,128)S(1)}, f32[8,4,32,128]{3,2,1,0:T(8,128)}, u32[]{:S(2)}) copy-start(f32[8,4,32,128]{3,2,1,0:T(8,128)} %param.3) | copy-start | bytes 1572868

commit v4 on v3

--- a/solution.py
+++ b/solution.py
@@ -41,7 +41,6 @@
     rads,
     stages,
     orbit,
-    remap,
     state,
     main,
     ghost_cols,
@@ -102,8 +101,8 @@
         for i in range(1, 8):
             amount = jnp.where(sub8 == i, orbit[8 * t + i], amount)
         shift[pl.ds(8 * t, 8), :] = amount
-    top = orbit[height - 1] + jnp.where(rad == rads - 1, remap[0], 0)
-    bottom = orbit[0] + jnp.where(rad == 0, total - remap[0], 0)
+    top = orbit[height - 1] + jnp.where(rad == rads - 1, orbit[height], 0)
+    bottom = orbit[0] + jnp.where(rad == 0, total - orbit[height], 0)
     amount = jnp.where(sub8 == 7, top, bottom)
     shift[pl.ds(height, 8), :] = jnp.where(amount >= total, amount - total, amount)
     out_cols[...] = jnp.zeros_like(out_cols)
@@ -532,10 +531,10 @@
     return outer, other_core, inner
 
 
-def whole_kernel(count, rads, orbit, remap, state, new, *scratch):
+def whole_kernel(count, rads, orbit, state, new, *scratch):
     landed, rest, work = scratch[:8], scratch[8:22], scratch[22:]
     stages = step_stages(count, *landed, new, *work)
-    move_kernel(count, rads, stages, orbit, remap, state, *landed, *rest)
+    move_kernel(count, rads, stages, orbit, state, *landed, *rest)
 
 
 def per_device(state, orbit_shift, remap_shift):
@@ -558,7 +557,6 @@
         functools.partial(whole_kernel, count, rads),
         out_shape=jax.ShapeDtypeStruct(state.shape, f32),
         in_specs=[
-            pl.BlockSpec(memory_space=pltpu.SMEM),
             pl.BlockSpec(memory_space=pltpu.SMEM),
             pl.BlockSpec(memory_space=pl.ANY),
         ],
@@ -603,7 +601,7 @@
             collective_id=0, has_side_effects=True, vmem_limit_bytes=24 * 1024 * 1024
         ),
         name="whole",
-    )(orbit_shift, remap_shift, state.reshape(fields * planes, height, width))
+    )(jnp.concatenate([orbit_shift, remap_shift]), state.reshape(fields * planes, height, width))
 
 
 def solution(mesh):

time: 39.2 us -> 38.7 us (0.987)
  local copies, waits for them, and re-layouts: 2.49 us -> 1.84 us
    unnamed x5, local copies, waits for them, and re-layouts: 2.49 us -> 1.84 us
where the time goes in v4:
time: 38.7 us; the launch traced here: 38.5 us
  Pallas kernels  35.9 us (93%)
  local copies, waits for them, and re-layouts  1.84 us (5%)
  between operations  0.68 us (2%)
    pallas_call x1, Pallas kernels, per_device(): pl.pallas_call(functools.partial(whole_kernel, count, rads), out_shape=ja...  35.9 us
    unnamed x5, local copies, waits for them, and re-layouts  1.84 us

profile of v4, /device:TPU:0, one launch (start us, length us, event | category | flops | bytes accessed | tf_op | source)
XLA Modules:
  0.0 38.5 jit_solution(1599508612712160948)
XLA Ops:
  0.0 0.0 copy-start.1
  0.7 0.0 copy-done.1
  0.7 0.1 pad_add_fusion.orbit
  0.8 0.0 copy-start
  0.8 1.0 %copy-done = f32[8,4,32,128]{3,2,1,0:T(8,128)S(1)} copy-done((f32[8,4,32,128]{3,2,1,0:T(8,128)S(1)}, f32[8,4,32,128]{3,2,1,0:T(8,128)}, u32[]{:S(2)}) %copy-start) | copy-done | bytes 524312
  1.8 35.9 %whole.1 = f32[8,4,32,128]{3,2,1,0:T(8,128)S(1)} custom-call(s32[33]{0:T(128)S(1)} %pad_add_fusion.orbit, f32[32,32,128]{2,1,0:T(8,128)S(1)} %bitcast.1), custom_call_target="tpu_custom_call" | custom-call | tf_op jit(solution)/shard_map/whole/pallas_call | solution.py:556
  37.7 0.8 %copy.6 = f32[8,4,32,128]{3,2,1,0:T(8,128)} copy(f32[8,4,32,128]{3,2,1,0:T(8,128)S(1)} %whole.1) | data formatting | bytes 1048576
Async XLA Ops:
  0.0 0.7 %copy-start.1 = (s32[32]{0:T(128)S(1)}, s32[32]{0:T(128)}, u32[]{:S(2)}) copy-start(s32[32]{0:T(128)} %param.4) | copy-start | bytes 388
  0.8 1.0 %copy-start = (f32[8,4,32,128]{3,2,1,0:T(8,128)S(1)}, f32[8,4,32,128]{3,2,1,0:T(8,128)}, u32[]{:S(2)}) copy-start(f32[8,4,32,128]{3,2,1,0:T(8,128)} %param.3) | copy-start | bytes 1572868
